TPU v7x, 32 devices: a whole 2x2x4 slice. The times are simulated.
32 devices in a mesh: groups: 2 (over x), tensor: 4 (over y, core), replica: 4 (over z).
Axes of the slice: x: 2, y: 2, z: 4, core: 2. Of those that a mesh axis runs over, the one named last changes fastest.
Arguments:
- normed_hidden_input: bfloat16 [2048, 8192], P(('groups', 'replica'), 'tensor'), parts along dimension 0, may hold values from -6 to 6
- attention_heads_context: bfloat16 [2048, 8192], P(('groups', 'replica'), 'tensor'), parts along dimension 0, may hold values from -6 to 6
- query_weight_matrix: bfloat16 [8192, 8192], P('tensor', 'replica'), may hold values from -0.0625 to 0.0625
- keyval_weight_matrix: bfloat16 [8192, 2048], P('tensor', 'replica'), may hold values from -0.0625 to 0.0625
- output_weight_matrix: bfloat16 [8192, 8192], P('tensor', 'replica'), may hold values from -0.0625 to 0.0625
- down_qkv: bfloat16 [128, 8192, 192], P(('groups', 'replica'), 'tensor'), parts along dimension 0, may hold values from -0.0625 to 0.0625
- down_out: bfloat16 [128, 8192, 64], P(('groups', 'replica'), 'tensor'), parts along dimension 0, may hold values from -0.0625 to 0.0625
- up_query: bfloat16 [128, 64, 8192], P(('groups', 'tensor'), None, 'replica'), parts along dimension 0, may hold values from -0.75 to 0.75
- up_keyval: bfloat16 [128, 64, 2048], P(('groups', 'tensor'), None, 'replica'), parts along dimension 0, may hold values from -0.75 to 0.75
- up_output: bfloat16 [128, 64, 8192], P(('groups', 'tensor'), None, 'replica'), parts along dimension 0, may hold values from -0.75 to 0.75
- seg_lengths: int32 [32], P('groups'), parts along dimension 0, may hold values from 1 to 256, 1024 in all
- seg_adapter: int32 [32], P('groups'), parts along dimension 0, may hold values from 0 to 63
- adapter_rank: int32 [128], P('groups'), parts along dimension 0, may hold values from 16 to 64
Outputs:
- query: bfloat16 [2048, 8192], P(('groups', 'tensor'), 'replica'), parts along dimension 0
- keyval: bfloat16 [2048, 2048], P(('groups', 'tensor'), 'replica'), parts along dimension 0
- adapted_output_matrix: bfloat16 [2048, 8192], P(('groups', 'tensor'), 'replica'), parts along dimension 0
There are 2 independent parts, one for each index of `groups`. A program takes and returns all parts, laid end to end along the dimension named above; an argument that names none is the same for every part. Nothing has to cross between parts.
Inputs may be any that keep to these rules, and one draw needn't show every extreme that they name: `seg_lengths`: 16 request lengths that sum to 1024; the longest is exactly 256. `seg_adapter`: an adapter index below 64 for each request. `adapter_rank`: each adapter's rank, at most 64.
All inputs are finite; a program needn't handle non-finite values.
Results may differ from a plain program's by a relative error of at most 0.0038.
Values may be sent and summed in bfloat16 or wider, within the bound.
A program may use at most 192 MiB of HBM per device.

v0:
```python
import jax
import jax.numpy as jnp
from jax import lax
from jax.sharding import PartitionSpec as P

KVD = 1024


def select_token_rows(array, segment_begin, count):
    return lax.dynamic_slice_in_dim(array, segment_begin, count, 0)


def segment_accumulate(accum, seg_index, seg_starts, seg_adapter, first, count, block, make_term):
    total_rows = accum.shape[0]

    def step(carry, segment):
        owner = seg_adapter[segment] - first
        is_local = jnp.logical_and(owner >= 0, owner < count)
        owner_safe = jnp.clip(owner, 0, count - 1)
        block_start = jnp.minimum(seg_starts[segment], total_rows - block)

        def apply(current):
            inside = (select_token_rows(seg_index, block_start, block) == segment)[:, None]
            term = make_term(owner_safe, block_start)
            updated = select_token_rows(current, block_start, block) + jnp.where(inside, term, 0.0)
            return lax.dynamic_update_slice_in_dim(current, updated, block_start, 0)

        return (lax.cond(is_local, apply, lambda current: current, carry), None)

    result, unused_value = lax.scan(step, accum, jnp.arange(seg_adapter.shape[0], dtype=jnp.int32))
    return result


def shards(
    normed_hidden_input,
    attention_heads_context,
    query_weight_matrix,
    keyval_weight_matrix,
    output_weight_matrix,
    down_qkv,
    down_out,
    up_query,
    up_keyval,
    up_output,
    seg_lengths,
    seg_adapter,
    adapter_rank,
):
    hidden_all, context_all = (
        lax.all_gather(normed_hidden_input, "replica", axis=0, tiled=True),
        lax.all_gather(attention_heads_context, "replica", axis=0, tiled=True),
    )
    total = hidden_all.shape[0]
    block = total // 4
    rank_width = up_query.shape[1]
    seg_ends = jnp.cumsum(seg_lengths)
    seg_starts = seg_ends - seg_lengths
    positions = jnp.arange(total, dtype=jnp.int32)
    seg_index = jnp.sum((positions[:, None] >= seg_ends[None, :]).astype(jnp.int32), axis=1)
    seg_hot = seg_index[:, None] == jnp.arange(seg_lengths.shape[0], dtype=jnp.int32)[None, :]
    adapter = jnp.sum(jnp.where(seg_hot, seg_adapter[None, :], 0), axis=1)
    adapter_hot = adapter[:, None] == jnp.arange(adapter_rank.shape[0], dtype=jnp.int32)[None, :]
    rank = jnp.sum(jnp.where(adapter_hot, adapter_rank[None, :], 0), axis=1)
    down_count = down_qkv.shape[0]
    down_first = lax.axis_index("replica") * down_count

    def down_term(owner, segment_begin):
        table_qkv = lax.dynamic_index_in_dim(down_qkv, owner, 0, keepdims=False)
        table_out = lax.dynamic_index_in_dim(down_out, owner, 0, keepdims=False)
        low_qkv = jnp.dot(
            select_token_rows(hidden_all, segment_begin, block),
            table_qkv,
            preferred_element_type=jnp.float32,
        )
        low_out = jnp.dot(
            select_token_rows(context_all, segment_begin, block),
            table_out,
            preferred_element_type=jnp.float32,
        )
        return jnp.concatenate([low_qkv, low_out], axis=1)

    low_part = segment_accumulate(
        jnp.zeros((total, 4 * rank_width), jnp.float32),
        seg_index,
        seg_starts,
        seg_adapter,
        down_first,
        down_count,
        block,
        down_term,
    )
    low_full = lax.psum(low_part, ("tensor", "replica"))
    columns = jnp.arange(rank_width, dtype=jnp.int32)
    keep = jnp.where(
        columns[None, :] < rank[:, None], 0.5 * rank_width / rank.astype(jnp.float32)[:, None], 0.0
    )
    rank_act = (low_full * jnp.tile(keep, (1, 4))).astype(jnp.bfloat16)
    up_count = up_query.shape[0]
    up_first = lax.axis_index("tensor") * up_count
    kv_width = up_keyval.shape[2]
    kv_start = lax.axis_index("replica") * kv_width
    rank_query = rank_act[:, :rank_width]
    rank_keyval = jnp.where(
        kv_start >= KVD,
        rank_act[:, 2 * rank_width : 3 * rank_width],
        rank_act[:, rank_width : 2 * rank_width],
    )
    rank_out = rank_act[:, 3 * rank_width :]
    query_column_count = query_weight_matrix.shape[1]
    query_keyval_columns = query_column_count + keyval_weight_matrix.shape[1]
    all_cols = query_keyval_columns + output_weight_matrix.shape[1]

    def up_term(owner, segment_begin):
        table_query = lax.dynamic_index_in_dim(up_query, owner, 0, keepdims=False)
        table_keyval = lax.dynamic_index_in_dim(up_keyval, owner, 0, keepdims=False)
        table_out = lax.dynamic_index_in_dim(up_output, owner, 0, keepdims=False)
        part_query = jnp.dot(
            select_token_rows(rank_query, segment_begin, block),
            table_query,
            preferred_element_type=jnp.float32,
        )
        part_keyval = jnp.dot(
            select_token_rows(rank_keyval, segment_begin, block),
            table_keyval,
            preferred_element_type=jnp.float32,
        )
        part_out = jnp.dot(
            select_token_rows(rank_out, segment_begin, block),
            table_out,
            preferred_element_type=jnp.float32,
        )
        return jnp.concatenate([part_query, part_keyval, part_out], axis=1)

    adapter_rows_joined = segment_accumulate(
        jnp.zeros((total, all_cols), jnp.float32),
        seg_index,
        seg_starts,
        seg_adapter,
        up_first,
        up_count,
        block,
        up_term,
    )
    segment_own_rows = total // lax.axis_size("tensor")
    segment_begin = jnp.int32(0)
    input_row_block = select_token_rows(
        hidden_all, segment_begin, lax.axis_size("tensor") * segment_own_rows
    )
    adapter_token_rows = select_token_rows(
        adapter_rows_joined, segment_begin, lax.axis_size("tensor") * segment_own_rows
    )
    query_part = (
        jnp.dot(input_row_block, query_weight_matrix, preferred_element_type=jnp.float32)
        + adapter_token_rows[:, :query_column_count]
    )
    keyval_part = (
        jnp.dot(input_row_block, keyval_weight_matrix, preferred_element_type=jnp.float32)
        + adapter_token_rows[:, query_column_count:query_keyval_columns]
    )
    qkv_sum = lax.psum_scatter(
        jnp.concatenate([query_part, keyval_part], axis=1),
        "tensor",
        scatter_dimension=0,
        tiled=True,
    )
    segment_begin = jnp.int32(0)
    out_sum = lax.psum_scatter(
        jnp.dot(
            select_token_rows(
                context_all, segment_begin, lax.axis_size("tensor") * segment_own_rows
            ),
            output_weight_matrix,
            preferred_element_type=jnp.float32,
        )
        + select_token_rows(
            adapter_rows_joined, segment_begin, lax.axis_size("tensor") * segment_own_rows
        )[:, query_keyval_columns:],
        "tensor",
        scatter_dimension=0,
        tiled=True,
    )
    return (
        qkv_sum[:, :query_column_count].astype(jnp.bfloat16),
        qkv_sum[:, query_column_count:].astype(jnp.bfloat16),
        out_sum.astype(jnp.bfloat16),
    )


def solution(mesh):
    in_specs = (
        P(("groups", "replica"), "tensor"),
        P(("groups", "replica"), "tensor"),
        P("tensor", "replica"),
        P("tensor", "replica"),
        P("tensor", "replica"),
        P(("groups", "replica"), "tensor", None),
        P(("groups", "replica"), "tensor", None),
        P(("groups", "tensor"), None, "replica"),
        P(("groups", "tensor"), None, "replica"),
        P(("groups", "tensor"), None, "replica"),
        P("groups"),
        P("groups"),
        P("groups"),
    )
    out_specs = (
        P(("groups", "tensor"), "replica"),
        P(("groups", "tensor"), "replica"),
        P(("groups", "tensor"), "replica"),
    )
    return jax.shard_map(shards, mesh=mesh, in_specs=in_specs, out_specs=out_specs, check_vma=False)
```

profile of v0, /device:TPU:0, one launch (start us, length us, event | category | flops | bytes accessed | tf_op | source)
XLA Modules:
  0.0 868.4 jit_solution(5166186166699560706)
XLA Ops:
  10.3 8.4 copy.30
  18.6 20.7 %copy.29 = bf16[16,2048,192]{2,1,0:T(8,128)(2,1)} copy(bf16[16,2048,192]{1,2,0:T(8,128)(2,1)} %param.26) | data formatting | bytes 25165824 | tf_op jit(solution)/shard_map/while | solution.py:30
  39.6 53.5 %all-gather.3.cloned.1.call-done = bf16[1024,2048]{1,0:T(8,128)(2,1)} async-done(((bf16[256,2048]{1,0:T(8,128)(2,1)}), bf16[1024,2048]{1,0:T(8,128)(2,1)}) %all-gather.3.cloned.1.call-update) | async-done | bytes 4194320 | tf_op jit(solution)/shard_map/all_gather | solution.py:50
  93.1 80.9 %all-gather.5.cloned.1.call-done = bf16[1024,2048]{1,0:T(8,128)(2,1)} async-done(((bf16[256,2048]{1,0:T(8,128)(2,1)}), bf16[1024,2048]{1,0:T(8,128)(2,1)}) %all-gather.5.cloned.1.call-update) | async-done | bytes 4194320 | tf_op jit(solution)/shard_map/all_gather | solution.py:51
  174.1 94.6 %while.26 = (s32[]{:T(128)}, f32[1024,256]{0,1:T(8,128)S(1)}, s32[16]{0:T(128)S(1)}, s32[16]{0:T(128)S(1)}, s32[]{:T(128)}, /*index=5*/s32[16]{0:T(128)S(1)}, s3...) while((s32[]{:T(128)}, f32[1024,256]{0,1:T(8,128)S(1)}, ...), condition=%wide.region_5.6_spmd, body=%wide.region_2.5_spmd.sunk | while | flops 268632320 | bytes 5244855 | solution.py:30
  191.7 8.4 conditional.4
  193.0 2.2 fusion
  195.2 1.8 fusion.2
  197.8 2.2 dynamic_update_slice.6
  207.1 8.4 conditional.4
  208.4 2.2 fusion
  210.6 1.8 fusion.2
  213.2 2.2 dynamic_update_slice.6
  229.5 7.2 conditional.4
  230.9 2.1 fusion
  233.0 1.8 fusion.2
  247.3 7.2 conditional.4
  248.6 2.1 fusion
  250.8 1.8 fusion.2
  261.5 7.2 conditional.4
  262.9 2.1 fusion
  265.0 1.8 fusion.2
  270.0 128.2 %all-reduce.2.cloned.1.call-done = f32[1024,256]{0,1:T(8,128)} async-done(((f32[1024,256]{0,1:T(8,128)}), f32[1024,256]{0,1:T(8,128)}) %all-reduce.2.cloned.1.call-update) | async-done | bytes 1048592 | tf_op jit(solution)/shard_map/psum | solution.py:92
  400.1 8.8 %broadcast_in_dim.83 = f32[1024,4608]{1,0:T(8,128)} broadcast(f32[]{:T(128)} %constant.93.clone.1), dimensions={} | broadcast | bytes 18874372 | tf_op jit(solution)/shard_map/broadcast_in_dim | solution.py:135
  408.9 176.9 %while.27 = (s32[]{:T(128)}, f32[1024,4608]{1,0:T(8,128)}, s32[16]{0:T(128)S(1)}, s32[16]{0:T(128)S(1)}, s32[]{:T(128)}, /*index=5*/s32[16]{0:T(128)S(1)}, s32[1...) while((s32[]{:T(128)}, f32[1024,4608]{1,0:T(8,128)}, ...), condition=%wide.region_12.13_spmd, body=%wide.region_9.12_spmd.sunk | while | flops 155713808 | bytes 29100000 | solution.py:30
  427.5 23.9 %conditional.5 = (f32[1024,4608]{1,0:T(8,128)}) conditional(s32[]{:T(128)} %convert_element_type.34, f32[1024,4608]{1,0:T(8,128)} %get-tuple-element.582, (s32[16]{0:T(128)S(1)}, s32[]{:T(128)}, f32[1024,4608]{1,0:T(8,128)}, s32[1024]{0:T(1024)S(1)}, s32[]{:T(128)}, /*index=5*/bf16[1024,64]{1,0:T(8,128)(2,1)S(1)}, s32[]{:T(128)}, ...), branch_computations={%region_10.10_spmd, %region_11.11_spmd} | conditional | flops 155713792 | bytes 29099650 | solution.py:28
  433.3 5.6 fusion.11
  438.9 12.5 %dynamic_update_slice.7 = f32[1024,4608]{1,0:T(8,128)} dynamic-update-slice(f32[1024,4608]{1,0:T(8,128)} %get-tuple-element.234, f32[256,4608]{1,0:T(8,128)} %fusion.11, s32[]{:T(128)S(6)} %select_n.65, s32[]{:T(128)} %constant.83.clone) | dynamic-update-slice | bytes 9437188 | tf_op jit(solution)/shard_map/while/body/eval_jaxpr/cond/branch_1_fun/dynamic_update_slice | solution.py:26
  458.8 23.9 %conditional.5 = (f32[1024,4608]{1,0:T(8,128)}) conditional(s32[]{:T(128)} %convert_element_type.34, f32[1024,4608]{1,0:T(8,128)} %get-tuple-element.582, (s32[16]{0:T(128)S(1)}, s32[]{:T(128)}, f32[1024,4608]{1,0:T(8,128)}, s32[1024]{0:T(1024)S(1)}, s32[]{:T(128)}, /*index=5*/bf16[1024,64]{1,0:T(8,128)(2,1)S(1)}, s32[]{:T(128)}, ...), branch_computations={%region_10.10_spmd, %region_11.11_spmd} | conditional | flops 155713792 | bytes 29099650 | solution.py:28
  464.6 5.6 fusion.11
  470.2 12.5 %dynamic_update_slice.7 = f32[1024,4608]{1,0:T(8,128)} dynamic-update-slice(f32[1024,4608]{1,0:T(8,128)} %get-tuple-element.234, f32[256,4608]{1,0:T(8,128)} %fusion.11, s32[]{:T(128)S(6)} %select_n.65, s32[]{:T(128)} %constant.83.clone) | dynamic-update-slice | bytes 9437188 | tf_op jit(solution)/shard_map/while/body/eval_jaxpr/cond/branch_1_fun/dynamic_update_slice | solution.py:26
  497.6 23.2 %conditional.5 = (f32[1024,4608]{1,0:T(8,128)}) conditional(s32[]{:T(128)} %convert_element_type.34, f32[1024,4608]{1,0:T(8,128)} %get-tuple-element.582, (s32[16]{0:T(128)S(1)}, s32[]{:T(128)}, f32[1024,4608]{1,0:T(8,128)}, s32[1024]{0:T(1024)S(1)}, s32[]{:T(128)}, /*index=5*/bf16[1024,64]{1,0:T(8,128)(2,1)S(1)}, s32[]{:T(128)}, ...), branch_computations={%region_10.10_spmd, %region_11.11_spmd} | conditional | flops 155713792 | bytes 29099650 | solution.py:28
  503.4 5.6 fusion.11
  509.0 11.8 %dynamic_update_slice.7 = f32[1024,4608]{1,0:T(8,128)} dynamic-update-slice(f32[1024,4608]{1,0:T(8,128)} %get-tuple-element.234, f32[256,4608]{1,0:T(8,128)} %fusion.11, s32[]{:T(128)S(6)} %select_n.65, s32[]{:T(128)} %constant.83.clone) | dynamic-update-slice | bytes 9437188 | tf_op jit(solution)/shard_map/while/body/eval_jaxpr/cond/branch_1_fun/dynamic_update_slice | solution.py:26
  531.9 23.2 %conditional.5 = (f32[1024,4608]{1,0:T(8,128)}) conditional(s32[]{:T(128)} %convert_element_type.34, f32[1024,4608]{1,0:T(8,128)} %get-tuple-element.582, (s32[16]{0:T(128)S(1)}, s32[]{:T(128)}, f32[1024,4608]{1,0:T(8,128)}, s32[1024]{0:T(1024)S(1)}, s32[]{:T(128)}, /*index=5*/bf16[1024,64]{1,0:T(8,128)(2,1)S(1)}, s32[]{:T(128)}, ...), branch_computations={%region_10.10_spmd, %region_11.11_spmd} | conditional | flops 155713792 | bytes 29099650 | solution.py:28
  537.7 5.6 fusion.11
  543.3 11.8 %dynamic_update_slice.7 = f32[1024,4608]{1,0:T(8,128)} dynamic-update-slice(f32[1024,4608]{1,0:T(8,128)} %get-tuple-element.234, f32[256,4608]{1,0:T(8,128)} %fusion.11, s32[]{:T(128)S(6)} %select_n.65, s32[]{:T(128)} %constant.83.clone) | dynamic-update-slice | bytes 9437188 | tf_op jit(solution)/shard_map/while/body/eval_jaxpr/cond/branch_1_fun/dynamic_update_slice | solution.py:26
  562.6 23.2 %conditional.5 = (f32[1024,4608]{1,0:T(8,128)}) conditional(s32[]{:T(128)} %convert_element_type.34, f32[1024,4608]{1,0:T(8,128)} %get-tuple-element.582, (s32[16]{0:T(128)S(1)}, s32[]{:T(128)}, f32[1024,4608]{1,0:T(8,128)}, s32[1024]{0:T(1024)S(1)}, s32[]{:T(128)}, /*index=5*/bf16[1024,64]{1,0:T(8,128)(2,1)S(1)}, s32[]{:T(128)}, ...), branch_computations={%region_10.10_spmd, %region_11.11_spmd} | conditional | flops 155713792 | bytes 29099650 | solution.py:28
  568.4 5.6 fusion.11
  574.0 11.8 %dynamic_update_slice.7 = f32[1024,4608]{1,0:T(8,128)} dynamic-update-slice(f32[1024,4608]{1,0:T(8,128)} %get-tuple-element.234, f32[256,4608]{1,0:T(8,128)} %fusion.11, s32[]{:T(128)S(6)} %select_n.65, s32[]{:T(128)} %constant.83.clone) | dynamic-update-slice | bytes 9437188 | tf_op jit(solution)/shard_map/while/body/eval_jaxpr/cond/branch_1_fun/dynamic_update_slice | solution.py:26
  585.8 15.7 %slice_add_fusion = f32[1024,2048]{1,0:T(8,128)} fusion(f32[1024,4608]{1,0:T(8,128)} %get-tuple-element.266, bf16[1024,2048]{1,0:T(8,128)(2,1)} %get-tuple-element.629, bf16[2048,2048]{1,0:T(8,128)(2,1)} %param.25), kind=kOutput, calls=%fused_computation.32 | convolution fusion | flops 8592031744 | bytes 29360128 | tf_op jit(solution)/shard_map/dot_general | solution.py:168
  601.8 6.6 slice_add_fusion.2
  608.4 14.5 %slice_add_fusion.1 = f32[1024,2048]{1,0:T(8,128)} fusion(f32[1024,4608]{1,0:T(8,128)} %get-tuple-element.266, bf16[1024,2048]{1,0:T(8,128)(2,1)S(1)} %copy-done.2, bf16[2048,2048]{1,0:T(8,128)(2,1)} %param.23), kind=kOutput, calls=%fused_computation.33 | convolution fusion | flops 8592031744 | bytes 29360128 | tf_op jit(solution)/shard_map/dot_general | solution.py:153
  622.9 9.0 %pad_maximum_fusion = f32[1024,2560]{1,0:T(8,128)} fusion(f32[1024,512]{1,0:T(8,128)} %slice_add_fusion.2, f32[1024,2048]{1,0:T(8,128)} %slice_add_fusion.1), kind=kLoop, calls=%fused_computation.31 | loop fusion | flops 2621440 | bytes 20971520 | tf_op jit(solution)/shard_map/concatenate | solution.py:161
  631.9 138.3 %reduce-scatter.5.cloned.1.call-done = f32[256,2048]{1,0:T(8,128)} async-done(((f32[1024,2048]{1,0:T(8,128)}), f32[256,2048]{1,0:T(8,128)}) %reduce-scatter.5.cloned.1.call-update) | async-done | bytes 2097168 | tf_op jit(solution)/shard_map/reduce_scatter | solution.py:167
  770.2 2.7 convert_element_type.27
  772.9 85.2 %reduce-scatter.3.cloned.1.call-done = f32[256,2560]{1,0:T(8,128)} async-done(((f32[1024,2560]{1,0:T(8,128)}), f32[256,2560]{1,0:T(8,128)}) %reduce-scatter.3.cloned.1.call-update) | async-done | bytes 2621456 | tf_op jit(solution)/shard_map/reduce_scatter | solution.py:160
  858.2 1.9 convert.4
  (168 shorter events, 82.6 us)
Async XLA Ops:
  7.2 594.6 %copy-start = (bf16[2048,512]{1,0:T(8,128)(2,1)S(1)}, bf16[2048,512]{1,0:T(8,128)(2,1)}, u32[]{:S(2)}) copy-start(bf16[2048,512]{1,0:T(8,128)(2,1)} %param.24) | copy-start | bytes 6291460
  7.2 85.9 %all-gather.3.cloned.1.call-start = ((), (), s32[]{:S(2)}) async-start(), calls=%async_computation.2 | async-start | bytes 5242880 | tf_op jit(solution)/shard_map/all_gather | solution.py:50
  7.9 166.1 %all-gather.5.cloned.1.call-start = ((), (), s32[]{:S(2)}) async-start(), calls=%async_computation.3 | async-start | bytes 5242880 | tf_op jit(solution)/shard_map/all_gather | solution.py:51
  8.7 389.5 %all-reduce.2.cloned.1.call-start = ((), (), s32[]{:S(2)}) async-start(), calls=%async_computation.4 | async-start | bytes 2097152 | tf_op jit(solution)/shard_map/psum | solution.py:92
  18.6 20.8 %copy-start.4 = (s32[16]{0:T(128)S(1)}, s32[16]{0:T(128)}, u32[]{:S(2)}) copy-start(s32[16]{0:T(128)} %param.32) | copy-start | bytes 196
  174.1 95.7 %copy-start.3 = (s32[64]{0:T(128)S(1)}, s32[64]{0:T(128)}, u32[]{:S(2)}) copy-start(s32[64]{0:T(128)} %param.33) | copy-start | bytes 772
  268.7 1.0 copy-start.1
  269.7 500.5 %reduce-scatter.5.cloned.1.call-start = ((), (), s32[]{:S(2)}) async-start(), calls=%async_computation.6 | async-start | bytes 10485760 | tf_op jit(solution)/shard_map/reduce_scatter | solution.py:167
  601.6 256.6 %reduce-scatter.3.cloned.1.call-start = ((), (), s32[]{:S(2)}) async-start(), calls=%async_computation.5 | async-start | bytes 13107200 | tf_op jit(solution)/shard_map/reduce_scatter | solution.py:160
  601.8 6.7 copy-start.2
Sparse Core Ops, SparseCore 0:
  9.6 83.4 all-gather.2
  94.6 79.2 all-gather.4
  269.9 128.2 all-reduce.1
  601.7 168.4 reduce-scatter.4
  772.8 85.2 reduce-scatter.2
where the time goes:
time: 854 us; the launch traced here: 868 us
  waiting for transfers between devices  488 us (57%)
  local copies, waits for them, and re-layouts  155 us (18%)
  loops' own time  84.7 us (10%)
  matrix products  75.6 us (9%)
  other arithmetic  51.5 us (6%)
  between operations  13.9 us (2%)
    reduce_scatter x1, waiting for transfers between devices, shards(): lax.psum_scatter(jnp.dot(select_token_rows(context_all, segment_begin, la...  138 us
    psum x1, waiting for transfers between devices, shards(): low_full = lax.psum(low_part, ('tensor', 'replica'))  128 us
    reduce_scatter x1, waiting for transfers between devices, shards(): lax.psum_scatter(jnp.concatenate([query_part, keyval_part], axis=1), 'ten...  85.2 us
    all_gather x1, waiting for transfers between devices, shards(): lax.all_gather(attention_heads_context, 'replica', axis=0, tiled=True)  80.9 us
    another operation x2, loops' own time, segment_accumulate(): lax.scan(step, accum, jnp.arange(seg_adapter.shape[0], dtype=jnp.int32))  77.4 us
    dynamic_update_slice x10, local copies, waits for them, and re-layouts, apply(): return lax.dynamic_update_slice_in_dim(current, updated, block_start, 0)  68.2 us
    all_gather x1, waiting for transfers between devices, shards(): lax.all_gather(normed_hidden_input, 'replica', axis=0, tiled=True)  53.5 us
    while x5, local copies, waits for them, and re-layouts, segment_accumulate(): lax.scan(step, accum, jnp.arange(seg_adapter.shape[0], dtype=jnp.int32))  29.6 us
  transfers between devices with their start and end apart: 5, of which 5 were waited for; matrix products, arithmetic and copies ran while one was open for 7% of the time, Pallas kernels for 0%

commit v1 on v0

v1 whole, which is shorter than its diff:
```python
import functools

import jax
import jax.numpy as jnp
from jax import lax
from jax.experimental import pallas as pl
from jax.experimental.pallas import tpu as pltpu
from jax.sharding import PartitionSpec as P

KVD = 1024


def low_kernel(first_ref, adapter_ref, x_ref, table_ref, low_ref):
    a = pl.program_id(0)

    @pl.when(a == 0)
    def _():
        low_ref[...] = jnp.zeros_like(low_ref)

    term = jnp.dot(x_ref[...], table_ref[0], preferred_element_type=jnp.float32)
    low_ref[...] += jnp.where(adapter_ref[...] == first_ref[0] + a, term, 0.0)


def low_rows(x, table, adapter, first):
    rows, depth = x.shape
    count, _, width = table.shape
    return pl.pallas_call(
        low_kernel,
        grid_spec=pltpu.PrefetchScalarGridSpec(
            num_scalar_prefetch=1,
            grid=(count,),
            in_specs=[
                pl.BlockSpec((rows, 1), lambda a, s: (0, 0)),
                pl.BlockSpec((rows, depth), lambda a, s: (0, 0)),
                pl.BlockSpec((1, depth, width), lambda a, s: (a, 0, 0)),
            ],
            out_specs=pl.BlockSpec((rows, width), lambda a, s: (0, 0)),
        ),
        out_shape=jax.ShapeDtypeStruct((rows, width), jnp.float32),
        compiler_params=pltpu.CompilerParams(vmem_limit_bytes=40 * 2**20),
        cost_estimate=pl.CostEstimate(
            flops=2 * rows * depth * width * count,
            bytes_accessed=2 * (rows * depth + count * depth * width),
            transcendentals=0,
        ),
    )(first, adapter[:, None], x, table)


def token_tables(seg_lengths, seg_adapter, adapter_rank, total, rank_width):
    seg_ends = jnp.cumsum(seg_lengths)
    positions = jnp.arange(total, dtype=jnp.int32)
    seg_index = jnp.sum((positions[:, None] >= seg_ends[None, :]).astype(jnp.int32), axis=1)
    seg_hot = seg_index[:, None] == jnp.arange(seg_lengths.shape[0], dtype=jnp.int32)[None, :]
    adapter = jnp.sum(jnp.where(seg_hot, seg_adapter[None, :], 0), axis=1)
    adapter_hot = adapter[:, None] == jnp.arange(adapter_rank.shape[0], dtype=jnp.int32)[None, :]
    rank = jnp.sum(jnp.where(adapter_hot, adapter_rank[None, :], 0), axis=1)
    columns = jnp.arange(rank_width, dtype=jnp.int32)
    keep = jnp.where(
        columns[None, :] < rank[:, None], 0.5 * rank_width / rank.astype(jnp.float32)[:, None], 0.0
    )
    return adapter, keep


def shards(h, c, wq, wkv, wo, dqkv, dout, upq, upkv, upo, seg_lengths, seg_adapter, adapter_rank):
    hidden = lax.all_gather(h, "replica", axis=0, tiled=True)
    context = lax.all_gather(c, "replica", axis=0, tiled=True)
    total = hidden.shape[0]
    r = upq.shape[1]
    adapter, keep = token_tables(seg_lengths, seg_adapter, adapter_rank, total, r)
    first_down = (lax.axis_index("replica") * dqkv.shape[0]).astype(jnp.int32)[None]
    up_count = upq.shape[0]
    owner = lax.axis_index("tensor") * up_count + jnp.arange(up_count * r, dtype=jnp.int32) // r
    mine = adapter[:, None] == owner[None, :]

    def part(x, w, ranks, up):
        spread = jnp.where(mine, jnp.tile(ranks, (1, up_count)), jnp.bfloat16(0))
        up2 = up.reshape(up_count * r, up.shape[2])
        return (
            jnp.dot(x, w, preferred_element_type=jnp.float32)
            + jnp.dot(spread, up2, preferred_element_type=jnp.float32)
        ).astype(jnp.bfloat16)

    def reduce_rows(x):
        return lax.psum_scatter(x, "tensor", scatter_dimension=0, tiled=True)

    low_qkv = lax.psum(low_rows(hidden, dqkv, adapter, first_down), ("tensor", "replica"))
    act = (low_qkv * jnp.tile(keep, (1, 3))).astype(jnp.bfloat16)
    kv_width = upkv.shape[2]
    kv_start = lax.axis_index("replica") * kv_width
    rank_kv = jnp.where(kv_start >= KVD, act[:, 2 * r :], act[:, r : 2 * r])
    query = reduce_rows(part(hidden, wq, act[:, :r], upq))
    keyval = reduce_rows(part(hidden, wkv, rank_kv, upkv))
    low_out = lax.psum(low_rows(context, dout, adapter, first_down), ("tensor", "replica"))
    act_out = (low_out * keep).astype(jnp.bfloat16)
    out = reduce_rows(part(context, wo, act_out, upo))
    return query, keyval, out


def solution(mesh):
    in_specs = (
        P(("groups", "replica"), "tensor"),
        P(("groups", "replica"), "tensor"),
        P("tensor", "replica"),
        P("tensor", "replica"),
        P("tensor", "replica"),
        P(("groups", "replica"), "tensor", None),
        P(("groups", "replica"), "tensor", None),
        P(("groups", "tensor"), None, "replica"),
        P(("groups", "tensor"), None, "replica"),
        P(("groups", "tensor"), None, "replica"),
        P("groups"),
        P("groups"),
        P("groups"),
    )
    out_specs = (P(("groups", "tensor"), "replica"),) * 3
    return jax.shard_map(shards, mesh=mesh, in_specs=in_specs, out_specs=out_specs, check_vma=False)
```

time: 854 us -> 434 us (0.51); the launches traced: 868 us -> 433 us
  waiting for transfers between devices: 488 us -> 274 us
  local copies, waits for them, and re-layouts: 155 us -> 40.9 us
  loops' own time: 84.7 us -> 0 us
  other arithmetic: 51.5 us -> 3.95 us
  Pallas kernels: 0 us -> 43.5 us
  matrix products: 75.6 us -> 55.1 us
    reduce_scatter x2 -> x3, waiting for transfers between devices: 224 us -> 69.5 us  [reduce_rows(): return lax.psum_scatter(x, 'tensor', scatter_dimension=0, tiled=True)]
    another operation x34 -> x0, loops' own time: 84.7 us -> none  [the longest x2 77.4 us: segment_accumulate(): lax.scan(step, accum, jnp.arange(seg_adapter.shape[0], dtype=jnp.int32))]
    dynamic_update_slice x10 -> x0, local copies, waits for them, and re-layouts: 68.2 us -> none  [apply(): return lax.dynamic_update_slice_in_dim(current, updated, block_start, 0)]
    dynamic_slice x74 -> x0, local copies, waits for them, and re-layouts: 44.3 us -> none  [the longest x32 19.7 us: step(): owner = seg_adapter[segment] - first]
    pallas_call x0 -> x2, Pallas kernels: none -> 43.5 us  [low_rows(): pl.pallas_call(low_kernel, grid_spec=pltpu.PrefetchScalarGridSpec(num_sca...]
    unnamed x10 -> x16, local copies, waits for them, and re-layouts: 0.99 us -> 36.9 us
    psum x1, waiting for transfers between devices: 128 us -> 94.1 us  [shards(): lax.psum(low_rows(hidden, dqkv, adapter, first_down), ('tensor', 'replica'))]
    while x5 -> x0, local copies, waits for them, and re-layouts: 29.6 us -> none  [segment_accumulate(): lax.scan(step, accum, jnp.arange(seg_adapter.shape[0], dtype=jnp.int32))]
  transfers between devices with their start and end apart: 5 -> 6, of which waited for: 5 -> 5; matrix products, arithmetic and copies ran while one was open for 7% -> 19% of each run, Pallas kernels for 0% -> 5%
where the time goes in v1:
time: 434 us; the launch traced here: 433 us
  waiting for transfers between devices  274 us (63%)
  matrix products  55.1 us (13%)
  Pallas kernels  43.5 us (10%)
  local copies, waits for them, and re-layouts  40.9 us (9%)
  between operations  14.3 us (3%)
    psum x1, waiting for transfers between devices, shards(): lax.psum(low_rows(hidden, dqkv, adapter, first_down), ('tensor', 'replica'))  94.1 us
    reduce_scatter x3, waiting for transfers between devices, reduce_rows(): return lax.psum_scatter(x, 'tensor', scatter_dimension=0, tiled=True)  69.5 us
    all_gather x1, waiting for transfers between devices, shards(): context = lax.all_gather(c, 'replica', axis=0, tiled=True)  56 us
    all_gather x1, waiting for transfers between devices, shards(): hidden = lax.all_gather(h, 'replica', axis=0, tiled=True)  53.2 us
    pallas_call x2, Pallas kernels, low_rows(): pl.pallas_call(low_kernel, grid_spec=pltpu.PrefetchScalarGridSpec(num_sca...  43.5 us
    unnamed x16, local copies, waits for them, and re-layouts  36.9 us
    dot_general x3, matrix products, part(): jnp.dot(x, w, preferred_element_type=jnp.float32)  32.5 us
    dot_general x3, matrix products, part(): jnp.dot(spread, up2, preferred_element_type=jnp.float32)  22.6 us
  transfers between devices with their start and end apart: 6, of which 5 were waited for; matrix products, arithmetic and copies ran while one was open for 19% of the time, Pallas kernels for 5%

profile of v1, /device:TPU:0, one launch (start us, length us, event | category | flops | bytes accessed | tf_op | source)
XLA Modules:
  0.0 432.5 jit_solution(9057003030276183911)
XLA Ops:
  7.2 0.0 copy-start
  7.2 0.0 all-gather.3.cloned.1.call-start
  7.2 0.7 all-gather.3.cloned.1.call-update
  7.9 0.0 all-gather.5.cloned.1.call-start
  8.0 0.7 all-gather.5.cloned.1.call-update
  8.7 0.0 all-reduce.3.cloned.1.call-start
  8.7 0.7 copy.32
  9.5 0.1 reduce
  9.6 0.1 convert_reduce_fusion
  9.7 0.7 select_reduce_fusion.1
  10.4 0.2 copy.33.adapter_ref
  10.7 20.8 %copy.34.table_ref = bf16[16,2048,192]{2,1,0:T(8,128)(2,1)} copy(bf16[16,2048,192]{1,2,0:T(8,128)(2,1)} %param.18) | data formatting | bytes 25165824 | tf_op args[5]
  31.4 8.4 %copy.40.table_ref = bf16[16,2048,64]{2,1,0:T(8,128)(2,1)} copy(bf16[16,2048,64]{1,2,0:T(8,128)(2,1)} %param.19) | data formatting | bytes 8388608 | tf_op args[6]
  39.8 53.2 %all-gather.3.cloned.1.call-done.x_ref = bf16[1024,2048]{1,0:T(8,128)(2,1)} async-done(((bf16[256,2048]{1,0:T(8,128)(2,1)}), bf16[1024,2048]{1,0:T(8,128)(2,1)}) %all-gather.3.cloned.1.call-update) | async-done | bytes 4194320 | tf_op jit(solution)/shard_map/all_gather | solution.py:65
  93.1 2.2 copy-done.4
  95.3 22.7 %shard_map.148 = f32[1024,192]{1,0:T(8,128)} custom-call(s32[1]{0:T(128)} %bitcast.1.first_ref, s32[1024,1]{1,0:T(8,128)S(1)} %copy.33.adapter_ref, bf16[1024,2048]{1,0:T(8,128)(2,1)S(1)} %copy-done.4, bf16[16,2048,192]{2,1,0:T(8,128)(2,1)} %copy.34.table_ref), custom_call_target="tpu_custom_call" | custom-call | flops 12884901888 | bytes 16777216 | tf_op jit(solution)/shard_map/pallas_call | solution.py:27
  117.9 56.0 %all-gather.5.cloned.1.call-done.x_ref = bf16[1024,2048]{1,0:T(8,128)(2,1)} async-done(((bf16[256,2048]{1,0:T(8,128)(2,1)}), bf16[1024,2048]{1,0:T(8,128)(2,1)}) %all-gather.5.cloned.1.call-update) | async-done | bytes 4194320 | tf_op jit(solution)/shard_map/all_gather | solution.py:66
  174.0 3.4 copy-done.2
  177.4 2.2 copy-done.3
  179.5 20.9 %shard_map.149 = f32[1024,64]{1,0:T(8,128)} custom-call(s32[1]{0:T(128)} %bitcast.1.first_ref, s32[1024,1]{1,0:T(8,128)S(1)} %copy.33.adapter_ref, bf16[1024,2048]{1,0:T(8,128)(2,1)S(1)} %copy-done.3, bf16[16,2048,64]{2,1,0:T(8,128)(2,1)S(1)} %copy-done.2), custom_call_target="tpu_custom_call" | custom-call | flops 4294967296 | bytes 8388608 | tf_op jit(solution)/shard_map/pallas_call | solution.py:27
  200.4 0.0 all-reduce.3.cloned.1.call-update
  200.5 0.0 reduce-scatter.6.cloned.1.call-start
  200.5 0.1 select_reduce_fusion
  200.7 94.1 %all-reduce.3.cloned.1.call-done = (f32[1024,192]{1,0:T(8,128)}, f32[1024,64]{1,0:T(8,128)}) async-done(((f32[1024,192]{1,0:T(8,128)}, f32[1024,64]{1,0:T(8,128)}), (f32[1024,192]{1,0:T(8,128)}, f32[1024,64]{1,0:T(8,128)})) %all-reduce.3.cloned.1.call-update) | async-done | bytes 1048592 | tf_op jit(solution)/shard_map/psum | solution.py:86
  294.8 1.4 multiply_convert_fusion.1
  296.2 0.2 copy.35
  296.4 1.0 tile.10
  297.4 1.5 copy.36
  298.8 1.3 multiply_convert_fusion
  300.2 0.1 slice_select_fusion
  300.3 0.1 copy.38
  300.4 2.7 fusion.2
  303.2 3.3 fusion.3
  306.5 0.0 reduce-scatter.6.cloned.1.call-update
  306.6 0.2 reduce-scatter.4.cloned.1.call-start
  306.8 14.6 %fusion.22 = f32[1024,2048]{1,0:T(8,128)} fusion(bf16[1024,2048]{1,0:T(8,128)(2,1)} %all-gather.3.cloned.1.call-done.x_ref, bf16[2048,2048]{1,0:T(8,128)(2,1)} %param.15), kind=kOutput, calls=%fused_computation.43 | convolution fusion | flops 8589934592 | bytes 20971520 | tf_op jit(solution)/shard_map/dot_general | solution.py:79
  321.4 0.1 copy.37
  321.5 9.9 %fusion.1 = bf16[1024,2048]{1,0:T(8,128)(2,1)} fusion(f32[1024,2048]{1,0:T(8,128)} %fusion.22, bf16[16,64,2048]{2,1,0:T(8,128)(2,1)} %param.20, s32[16,64]{1,0:T(8,128)S(1)} %fusion.17, s32[1024]{0:T(1024)S(1)} %select_reduce_fusion.1, bf16[1024,64]{0,1:T(8,128)(2,1)S(1)} %copy.37), kind=kOutput, calls=%fused_computation.3 | convolution fusion | flops 4301258752 | bytes 16916480 | tf_op jit(solution)/shard_map/dot_general | solution.py:80
  331.4 0.0 reduce-scatter.4.cloned.1.call-update
  331.4 0.0 reduce-scatter.8.cloned.1.call-start
  331.4 14.6 %fusion.23 = f32[1024,2048]{1,0:T(8,128)} fusion(bf16[1024,2048]{1,0:T(8,128)(2,1)} %all-gather.5.cloned.1.call-done.x_ref, bf16[2048,2048]{1,0:T(8,128)(2,1)} %param.17), kind=kOutput, calls=%fused_computation.44 | convolution fusion | flops 8589934592 | bytes 20971520 | tf_op jit(solution)/shard_map/dot_general | solution.py:79
  346.0 0.1 copy.41
  346.2 0.0 copy-start.1
  346.2 10.0 %fusion = bf16[1024,2048]{1,0:T(8,128)(2,1)} fusion(f32[1024,2048]{1,0:T(8,128)} %fusion.23, bf16[16,64,2048]{2,1,0:T(8,128)(2,1)} %param.22, s32[16,64]{1,0:T(8,128)S(1)} %fusion.17, s32[1024]{0:T(1024)S(1)} %select_reduce_fusion.1, bf16[1024,64]{0,1:T(8,128)(2,1)S(1)} %copy.41), kind=kOutput, calls=%fused_computation.1 | convolution fusion | flops 4301258752 | bytes 16916480 | tf_op jit(solution)/shard_map/dot_general | solution.py:80
  356.2 0.0 reduce-scatter.8.cloned.1.call-update
  356.2 0.0 reduce-scatter.6.cloned.1.call-done
  356.2 22.0 %reduce-scatter.4.cloned.1.call-done = bf16[256,2048]{1,0:T(8,128)(2,1)} async-done(((bf16[1024,2048]{1,0:T(8,128)(2,1)}), bf16[256,2048]{1,0:T(8,128)(2,1)}) %reduce-scatter.4.cloned.1.call-update) | async-done | bytes 1048592 | tf_op jit(solution)/shard_map/reduce_scatter | solution.py:84
  378.2 47.5 %reduce-scatter.8.cloned.1.call-done = bf16[256,2048]{1,0:T(8,128)(2,1)} async-done(((bf16[1024,2048]{1,0:T(8,128)(2,1)}), bf16[256,2048]{1,0:T(8,128)(2,1)}) %reduce-scatter.8.cloned.1.call-update) | async-done | bytes 1048592 | tf_op jit(solution)/shard_map/reduce_scatter | solution.py:84
  (12 shorter events, 0.1 us)
Async XLA Ops:
  7.2 296.0 %copy-start = (bf16[2048,512]{1,0:T(8,128)(2,1)S(1)}, bf16[2048,512]{1,0:T(8,128)(2,1)}, u32[]{:S(2)}) copy-start(bf16[2048,512]{1,0:T(8,128)(2,1)} %param.16) | copy-start | bytes 6291460
  7.2 85.9 %all-gather.3.cloned.1.call-start = ((), (), s32[]{:S(2)}) async-start(), calls=%async_computation.3 | async-start | bytes 5242880 | tf_op jit(solution)/shard_map/all_gather | solution.py:65
  7.9 166.1 %all-gather.5.cloned.1.call-start = ((), (), s32[]{:S(2)}) async-start(), calls=%async_computation.6 | async-start | bytes 5242880 | tf_op jit(solution)/shard_map/all_gather | solution.py:66
  8.7 286.1 %all-reduce.3.cloned.1.call-start = ((), (), s32[]{:S(2)}) async-start(), calls=%async_computation.8 | async-start | bytes 3145728 | tf_op jit(solution)/shard_map/psum | solution.py:86
  93.1 2.2 copy-start.4
  174.0 3.4 copy-start.2
  177.4 2.2 copy-start.3
  179.5 21.0 %copy-start.6 = (s32[64]{0:T(128)S(1)}, s32[64]{0:T(128)}, u32[]{:S(2)}) copy-start(s32[64]{0:T(128)} %param.25) | copy-start | bytes 772
  200.5 155.8 %reduce-scatter.6.cloned.1.call-start = ((), (), s32[]{:S(2)}) async-start(), calls=%async_computation.5 | async-start | bytes 1310720 | tf_op jit(solution)/shard_map/reduce_scatter | solution.py:84
  300.4 2.8 copy-start.5
  306.6 71.6 %reduce-scatter.4.cloned.1.call-start = ((), (), s32[]{:S(2)}) async-start(), calls=%async_computation.4 | async-start | bytes 5242880 | tf_op jit(solution)/shard_map/reduce_scatter | solution.py:84
  331.4 94.3 %reduce-scatter.8.cloned.1.call-start = ((), (), s32[]{:S(2)}) async-start(), calls=%async_computation.7 | async-start | bytes 5242880 | tf_op jit(solution)/shard_map/reduce_scatter | solution.py:84
  346.2 79.5 %copy-start.1 = (bf16[2048,512]{1,0:T(8,128)(2,1)S(1)}, bf16[2048,512]{1,0:T(8,128)(2,1)}, u32[]{:S(2)}) copy-start(bf16[2048,512]{1,0:T(8,128)(2,1)} %param.16) | copy-start | bytes 6291460
Sparse Core Ops, SparseCore 0:
  9.6 83.4 all-gather.2
  94.6 79.2 all-gather.4
  200.6 94.1 all-reduce.2
  306.7 23.7 reduce-scatter.5
  333.6 44.5 reduce-scatter.3
  381.1 44.4 reduce-scatter.7

commit v2 on v1

v2 whole, which is shorter than its diff:
```python
import functools

import jax
import jax.numpy as jnp
from jax import lax
from jax.experimental import pallas as pl
from jax.experimental.pallas import tpu as pltpu
from jax.sharding import PartitionSpec as P

KVD = 1024
PIECES = 1
OUT_CHUNKS = 2
TRANSPOSED = (((1,), (1,)), ((), ()))


def low_kernel(first_ref, adapter_ref, x_ref, table_ref, low_ref):
    step = pl.program_id(0)
    together, width, depth = table_ref.shape

    @pl.when(step == 0)
    def _():
        low_ref[...] = jnp.zeros_like(low_ref)

    term = lax.dot_general(
        x_ref[...],
        table_ref[...].reshape(together * width, depth),
        TRANSPOSED,
        preferred_element_type=jnp.float32,
    )
    adapter = adapter_ref[...]
    low = low_ref[...]
    for i in range(together):
        chosen = adapter == first_ref[0] + step * together + i
        low = low + jnp.where(chosen, term[:, i * width : (i + 1) * width], 0.0)
    low_ref[...] = low


def low_rows(x, table, adapter, first):
    rows, depth = x.shape
    count, width, _ = table.shape
    together = min(count, max(1, 256 // width))
    return pl.pallas_call(
        low_kernel,
        grid_spec=pltpu.PrefetchScalarGridSpec(
            num_scalar_prefetch=1,
            grid=(count // together,),
            in_specs=[
                pl.BlockSpec((rows, 1), lambda a, s: (0, 0)),
                pl.BlockSpec((rows, depth), lambda a, s: (0, 0)),
                pl.BlockSpec((together, width, depth), lambda a, s: (a, 0, 0)),
            ],
            out_specs=pl.BlockSpec((rows, width), lambda a, s: (0, 0)),
        ),
        out_shape=jax.ShapeDtypeStruct((rows, width), jnp.float32),
        compiler_params=pltpu.CompilerParams(vmem_limit_bytes=56 * 2**20),
        cost_estimate=pl.CostEstimate(
            flops=2 * rows * depth * width * count,
            bytes_accessed=2 * (rows * depth + count * depth * width),
            transcendentals=0,
        ),
    )(first, adapter, x, table)


def act_kernel(
    nt, nz, low_ref, keep_ref, act_ref, near, pair, cross, mine, far,
    s1, r1, s2, r2, s3, r3, s4, r4, s5, r5,
):
    t, z = lax.axis_index("tensor"), lax.axis_index("replica")
    ny = nt // 2
    y, core = t // 2, lax.rem(t, 2)
    rows, width = mine.shape
    partner = {"tensor": t + 1 - 2 * core}
    columns = [{"tensor": 2 * lax.rem(y + d, ny) + core} for d in range(1, ny)]
    planes = [{"replica": lax.rem(z + d, nz)} for d in range(1, nz)]
    barrier = pltpu.get_barrier_semaphore()
    for peer in [partner] + columns + planes:
        pl.semaphore_signal(barrier, inc=1, device_id=peer)
    pl.semaphore_wait(barrier, 1 + len(columns) + len(planes))

    def block(index):
        return pl.ds(pl.multiple_of(index * rows, rows), rows)

    def send_all(jobs, sends, recvs):
        copies = [
            pltpu.make_async_remote_copy(src, dst, sends.at[i], recvs.at[i], device_id=peer)
            for i, (src, dst, peer) in enumerate(jobs)
        ]
        for copy in copies:
            copy.start()
        for copy in copies:
            copy.wait()

    send_all(
        [(low_ref.at[block(2 * j + 1 - core)], near.at[j], partner) for j in range(ny)], s1, r1
    )
    for j in range(ny):
        pair[j] = low_ref[block(2 * j + core), :] + near[j]
    send_all(
        [
            (pair.at[lax.rem(y + d, ny)], cross.at[d - 1], columns[d - 1])
            for d in range(1, ny)
        ],
        s2,
        r2,
    )
    total = pair[y]
    for d in range(1, ny):
        total = total + cross[d - 1]
    keep = keep_ref[block(t), :]
    own = (total * jnp.concatenate([keep] * (width // keep.shape[1]), axis=1)).astype(jnp.bfloat16)
    mine[...] = own
    send_all([(mine, far.at[i], peer) for i, peer in enumerate(planes)], s3, r3)
    total = own.astype(jnp.float32)
    for d in range(1, nz):
        total = total + far[d - 1].astype(jnp.float32)
    act_ref[block(t), :] = total.astype(jnp.bfloat16)
    send_all([(act_ref.at[block(t)], act_ref.at[block(t)], peer) for peer in columns], s4, r4)
    send_all(
        [
            (act_ref.at[block(2 * j + core)], act_ref.at[block(2 * j + core)], partner)
            for j in range(ny)
        ],
        s5,
        r5,
    )


def rank_rows(low, keep, nt, nz, collective_id):
    total, width = low.shape
    rows = total // nt
    vmem = pl.BlockSpec(memory_space=pltpu.VMEM)
    ny = nt // 2
    pairs, across, planes = (pltpu.SemaphoreType.DMA((n,)) for n in (ny, ny - 1, nz - 1))
    return pl.pallas_call(
        functools.partial(act_kernel, nt, nz),
        in_specs=[vmem, vmem],
        out_specs=vmem,
        out_shape=jax.ShapeDtypeStruct((total, width), jnp.bfloat16),
        scratch_shapes=[
            pltpu.VMEM((ny, rows, width), jnp.float32),
            pltpu.VMEM((ny, rows, width), jnp.float32),
            pltpu.VMEM((ny - 1, rows, width), jnp.float32),
            pltpu.VMEM((rows, width), jnp.bfloat16),
            pltpu.VMEM((nz - 1, rows, width), jnp.bfloat16),
            pairs, pairs, across, across, planes, planes, across, across, pairs, pairs,
        ],
        compiler_params=pltpu.CompilerParams(
            collective_id=collective_id, has_side_effects=True, vmem_limit_bytes=16 * 2**20
        ),
        cost_estimate=pl.CostEstimate(
            flops=0, bytes_accessed=40 * 2**20, transcendentals=0
        ),
    )(low, keep)


def direct_act_kernel(
    nt, nz, low_ref, keep_ref, act_ref, near, mine, far, s1, r1, s2, r2, s3, r3
):
    t, z = lax.axis_index("tensor"), lax.axis_index("replica")
    rows, width = mine.shape
    barrier = pltpu.get_barrier_semaphore()
    for d in range(1, nt):
        pl.semaphore_signal(barrier, inc=1, device_id={"tensor": lax.rem(t + d, nt)})
    for d in range(1, nz):
        pl.semaphore_signal(barrier, inc=1, device_id={"replica": lax.rem(z + d, nz)})
    pl.semaphore_wait(barrier, nt + nz - 2)

    def block(index):
        return pl.ds(pl.multiple_of(index * rows, rows), rows)

    copies = []
    for d in range(1, nt):
        peer = lax.rem(t + d, nt)
        copies.append(
            pltpu.make_async_remote_copy(
                low_ref.at[block(peer)], near.at[d - 1], s1.at[d - 1], r1.at[d - 1],
                device_id={"tensor": peer},
            )
        )
        copies[-1].start()
    total = low_ref[block(t), :]
    for d in range(1, nt):
        copies[d - 1].wait()
        total = total + near[d - 1]
    keep = keep_ref[block(t), :]
    own = (total * jnp.concatenate([keep] * (width // keep.shape[1]), axis=1)).astype(jnp.bfloat16)
    mine[...] = own

    copies = []
    for d in range(1, nz):
        peer = lax.rem(z + d, nz)
        copies.append(
            pltpu.make_async_remote_copy(
                mine, far.at[d - 1], s2.at[d - 1], r2.at[d - 1], device_id={"replica": peer}
            )
        )
        copies[-1].start()
    total = own.astype(jnp.float32)
    for d in range(1, nz):
        copies[d - 1].wait()
        total = total + far[d - 1].astype(jnp.float32)
    act_ref[block(t), :] = total.astype(jnp.bfloat16)

    copies = []
    for d in range(1, nt):
        peer = lax.rem(t + d, nt)
        copies.append(
            pltpu.make_async_remote_copy(
                act_ref.at[block(t)], act_ref.at[block(t)], s3.at[d - 1], r3.at[d - 1],
                device_id={"tensor": peer},
            )
        )
        copies[-1].start()
    for copy in copies:
        copy.wait()


def direct_rank_rows(low, keep, nt, nz, collective_id):
    total, width = low.shape
    rows = total // nt
    vmem = pl.BlockSpec(memory_space=pltpu.VMEM)
    near, far = pltpu.SemaphoreType.DMA((nt - 1,)), pltpu.SemaphoreType.DMA((nz - 1,))
    return pl.pallas_call(
        functools.partial(direct_act_kernel, nt, nz),
        in_specs=[vmem, vmem],
        out_specs=vmem,
        out_shape=jax.ShapeDtypeStruct((total, width), jnp.bfloat16),
        scratch_shapes=[
            pltpu.VMEM((nt - 1, rows, width), jnp.float32),
            pltpu.VMEM((rows, width), jnp.bfloat16),
            pltpu.VMEM((nz - 1, rows, width), jnp.bfloat16),
            near, near, far, far, near, near,
        ],
        compiler_params=pltpu.CompilerParams(
            collective_id=collective_id, has_side_effects=True, vmem_limit_bytes=16 * 2**20
        ),
        cost_estimate=pl.CostEstimate(
            flops=0, bytes_accessed=40 * 2**20, transcendentals=0
        ),
    )(low, keep)


def part_kernel(first_ref, adapter_ref, x_ref, rank_ref, w_ref, up_ref, out_ref, spread_ref):
    @pl.when(pl.program_id(0) == 0)
    def _():
        rank_width = rank_ref.shape[1]
        rows, wide = spread_ref.shape
        row = lax.broadcasted_iota(jnp.int32, (rank_width, wide), 0)
        column = lax.broadcasted_iota(jnp.int32, (rank_width, wide), 1)
        repeat = jnp.where(column % rank_width == row, 1.0, 0.0).astype(jnp.bfloat16)
        tiled = jnp.dot(rank_ref[...], repeat, preferred_element_type=jnp.float32)
        owner = first_ref[0] + lax.broadcasted_iota(jnp.int32, (rows, wide), 1) // rank_width
        spread_ref[...] = jnp.where(adapter_ref[...] == owner, tiled, 0.0).astype(jnp.bfloat16)

    out_ref[...] = (
        jnp.dot(x_ref[...], w_ref[...], preferred_element_type=jnp.float32)
        + jnp.dot(spread_ref[...], up_ref[...], preferred_element_type=jnp.float32)
    ).astype(jnp.bfloat16)


def part_rows(x, w, ranks, up, adapter, first, chunk=0, chunks=1):
    rows, depth = x.shape
    columns = w.shape[1] // chunks
    count, rank_width, _ = up.shape
    wide = count * rank_width
    tile = min(512, columns)
    begin = chunk * columns // tile
    return pl.pallas_call(
        part_kernel,
        grid_spec=pltpu.PrefetchScalarGridSpec(
            num_scalar_prefetch=1,
            grid=(columns // tile,),
            in_specs=[
                pl.BlockSpec((rows, 1), lambda n, s: (0, 0)),
                pl.BlockSpec((rows, depth), lambda n, s: (0, 0)),
                pl.BlockSpec((rows, rank_width), lambda n, s: (0, 0)),
                pl.BlockSpec((depth, tile), lambda n, s: (0, begin + n)),
                pl.BlockSpec((wide, tile), lambda n, s: (0, begin + n)),
            ],
            out_specs=pl.BlockSpec((rows, tile), lambda n, s: (0, n)),
            scratch_shapes=[pltpu.VMEM((rows, wide), jnp.bfloat16)],
        ),
        out_shape=jax.ShapeDtypeStruct((rows, columns), jnp.bfloat16),
        compiler_params=pltpu.CompilerParams(vmem_limit_bytes=56 * 2**20),
        cost_estimate=pl.CostEstimate(
            flops=2 * rows * (depth + wide) * columns,
            bytes_accessed=2 * (rows * depth + (depth + wide) * columns + rows * columns),
            transcendentals=0,
        ),
    )(first, adapter, x, ranks, w, up.reshape(wide, up.shape[2]))


def token_tables(seg_lengths, seg_adapter, adapter_rank, total, rank_width):
    seg_ends = jnp.cumsum(seg_lengths)
    positions = jnp.arange(total, dtype=jnp.int32)
    seg_index = jnp.sum((positions[:, None] >= seg_ends[None, :]).astype(jnp.int32), axis=1)
    seg_hot = seg_index[:, None] == jnp.arange(seg_lengths.shape[0], dtype=jnp.int32)[None, :]
    adapter = jnp.sum(jnp.where(seg_hot, seg_adapter[None, :], 0), axis=1)
    adapter_hot = adapter[:, None] == jnp.arange(adapter_rank.shape[0], dtype=jnp.int32)[None, :]
    rank = jnp.sum(jnp.where(adapter_hot, adapter_rank[None, :], 0), axis=1)
    columns = jnp.arange(rank_width, dtype=jnp.int32)
    keep = jnp.where(
        columns[None, :] < rank[:, None], 0.5 * rank_width / rank.astype(jnp.float32)[:, None], 0.0
    )
    return adapter, keep


def reduce_rows(x, nt):
    if nt != 4:
        out = lax.psum_scatter(x, "tensor", scatter_dimension=0, tiled=True)
        return out, out
    t = lax.axis_index("tensor")
    core, y = t % 2, t // 2
    x = x.reshape(2, 2, x.shape[0] // 4, x.shape[1])
    keep = lax.dynamic_index_in_dim(x, core, 1, keepdims=False)
    give = lax.dynamic_index_in_dim(x, 1 - core, 1, keepdims=False)
    got = lax.ppermute(give, "tensor", [(0, 1), (1, 0), (2, 3), (3, 2)])

    def pair(index):
        a = lax.dynamic_index_in_dim(keep, index, 0, keepdims=False)
        b = lax.dynamic_index_in_dim(got, index, 0, keepdims=False)
        return a.astype(jnp.float32) + b.astype(jnp.float32)

    give = pair(1 - y).astype(jnp.bfloat16)
    got2 = lax.ppermute(give, "tensor", [(0, 2), (2, 0), (1, 3), (3, 1)])
    return (pair(y) + got2.astype(jnp.float32)).astype(jnp.bfloat16), give


def shards(nt, nz, h, c, wq, wkv, wo, dqkv, dout, upq, upkv, upo, seg_lengths, seg_adapter, adapter_rank):
    total = h.shape[0] * nz
    depth = h.shape[1]
    r = upq.shape[1]
    sub = nt // nz
    rows = total // nt // PIECES

    def local_piece(x, p):
        return x.reshape(sub, PIECES, rows, depth)[:, p].reshape(sub * rows, depth)

    adapter, keep = token_tables(seg_lengths, seg_adapter, adapter_rank, total, r)
    adapter = adapter.reshape(nt, PIECES, rows)
    keep = keep.reshape(nt, PIECES, rows, r)
    adapters = [adapter[:, p].reshape(nt * rows, 1) for p in range(PIECES)]
    keeps = [keep[:, p].reshape(nt * rows, r) for p in range(PIECES)]
    first_down = (lax.axis_index("replica") * dqkv.shape[0]).astype(jnp.int32)[None]
    first_up = (lax.axis_index("tensor") * upq.shape[0]).astype(jnp.int32)[None]
    table_qkv, table_out = jnp.swapaxes(dqkv, 1, 2), jnp.swapaxes(dout, 1, 2)
    is_value = lax.axis_index("replica") * upkv.shape[2] >= KVD

    gathered = []
    for x, p in [(h, p) for p in range(PIECES)] + [(c, p) for p in range(PIECES)]:
        piece = local_piece(x, p)
        if gathered:
            piece, gathered[-1] = lax.optimization_barrier((piece, gathered[-1]))
        gathered.append(lax.all_gather(piece, "replica", axis=0, tiled=True))

    queries, keyvals, outs = [], [], []
    given, reduced = (), ((), ())
    for piece in range(2 * PIECES):
        p = piece % PIECES
        adapter = adapters[p]
        x = lax.optimization_barrier((gathered[piece], given, reduced[0]))[0]
        if piece < PIECES:
            low = low_rows(x, table_qkv, adapter, first_down)
            act = rank_rows(low, keeps[p], nt, nz, piece)
            rank_kv = jnp.where(is_value, act[:, 2 * r :], act[:, r : 2 * r])
            query = part_rows(x, wq, act[:, :r], upq, adapter, first_up)
            keyval = part_rows(x, wkv, rank_kv, upkv, adapter, first_up)
            query, given_query = reduce_rows(query, nt)
            keyval, given_keyval = reduce_rows(keyval, nt)
            queries.append(query)
            keyvals.append(keyval)
            given, reduced = (given_query, given_keyval), (reduced[1], (query, keyval))
        else:
            low = low_rows(x, table_out, adapter, first_down)
            act = direct_rank_rows(low, keeps[p], nt, nz, piece)
            act = lax.optimization_barrier((act, reduced[1][0]))[0]
            chunks = []
            for chunk in range(OUT_CHUNKS):
                if chunks:
                    act = lax.optimization_barrier((act, chunks[-1][1], reduced[1][1]))[0]
                part = part_rows(x, wo, act, upo, adapter, first_up, chunk, OUT_CHUNKS)
                chunks.append(reduce_rows(part, nt))
            given = tuple(sent for _, sent in chunks)
            outs.append(jnp.concatenate([out for out, _ in chunks], axis=1))
            reduced = (reduced[1], (outs[-1],))
    return tuple(jnp.concatenate(pieces, axis=0) for pieces in (queries, keyvals, outs))


def solution(mesh):
    in_specs = (
        P(("groups", "replica"), "tensor"),
        P(("groups", "replica"), "tensor"),
        P("tensor", "replica"),
        P("tensor", "replica"),
        P("tensor", "replica"),
        P(("groups", "replica"), "tensor", None),
        P(("groups", "replica"), "tensor", None),
        P(("groups", "tensor"), None, "replica"),
        P(("groups", "tensor"), None, "replica"),
        P(("groups", "tensor"), None, "replica"),
        P("groups"),
        P("groups"),
        P("groups"),
    )
    out_specs = (P(("groups", "tensor"), "replica"),) * 3
    body = functools.partial(shards, mesh.shape["tensor"], mesh.shape["replica"])
    return jax.shard_map(body, mesh=mesh, in_specs=in_specs, out_specs=out_specs, check_vma=False)
```

time: 434 us -> 322 us (0.74)
  waiting for transfers between devices: 274 us -> 128 us
  Pallas kernels: 43.5 us -> 146 us
  matrix products: 55.1 us -> 0 us
  local copies, waits for them, and re-layouts: 40.9 us -> 12.7 us
  other arithmetic: 3.95 us -> 13.3 us
  starting transfers between devices: 0.42 us -> 6.84 us
    pallas_call x0 -> x6, Pallas kernels: none -> 113 us  [the longest x4 50.9 us: part_rows(): pl.pallas_call(part_kernel, grid_spec=pltpu.PrefetchScalarGridSpec(num_sc...]
    psum x1 -> x0, waiting for transfers between devices: 94.1 us -> none  [shards(): lax.psum(low_rows(hidden, dqkv, adapter, first_down), ('tensor', 'replica'))]
    reduce_scatter x3 -> x0, waiting for transfers between devices: 69.5 us -> none  [reduce_rows(): return lax.psum_scatter(x, 'tensor', scatter_dimension=0, tiled=True)]
    dot_general x6 -> x0, matrix products: 55.1 us -> none  [the longest x3 32.5 us: part(): jnp.dot(x, w, preferred_element_type=jnp.float32)]
    ppermute x0 -> x8, waiting for transfers between devices: none -> 46.3 us  [the longest x4 39 us: reduce_rows(): got2 = lax.ppermute(give, 'tensor', [(0, 2), (2, 0), (1, 3), (3, 1)])]
    unnamed x16 -> x10, local copies, waits for them, and re-layouts: 36.9 us -> 2.97 us
    all_gather x2, waiting for transfers between devices: 109 us -> 81.2 us  [shards(): gathered.append(lax.all_gather(piece, 'replica', axis=0, tiled=True))]
    pallas_call x2, Pallas kernels: 43.5 us -> 33.3 us  [low_rows(): pl.pallas_call(low_kernel, grid_spec=pltpu.PrefetchScalarGridSpec(num_sca...]
  transfers between devices with their start and end apart: 6 -> 10, of which waited for: 5 -> 8; matrix products, arithmetic and copies ran while one was open for 19% -> 6% of each run, Pallas kernels for 5% -> 27%
where the time goes in v2:
time: 322 us
  Pallas kernels  146 us (45%)
  waiting for transfers between devices  128 us (40%)
  between operations  14.2 us (4%)
  other arithmetic  13.3 us (4%)
  local copies, waits for them, and re-layouts  12.7 us (4%)
  starting transfers between devices  6.84 us (2%)
    all_gather x2, waiting for transfers between devices, shards(): gathered.append(lax.all_gather(piece, 'replica', axis=0, tiled=True))  81.2 us
    pallas_call x4, Pallas kernels, part_rows(): pl.pallas_call(part_kernel, grid_spec=pltpu.PrefetchScalarGridSpec(num_sc...  50.9 us
    ppermute x4, waiting for transfers between devices, reduce_rows(): got2 = lax.ppermute(give, 'tensor', [(0, 2), (2, 0), (1, 3), (3, 1)])  39 us
    pallas_call x1, Pallas kernels, rank_rows(): pl.pallas_call(functools.partial(act_kernel, nt, nz), in_specs=[vmem, vme...  34.1 us
    pallas_call x2, Pallas kernels, low_rows(): pl.pallas_call(low_kernel, grid_spec=pltpu.PrefetchScalarGridSpec(num_sca...  33.3 us
    pallas_call x1, Pallas kernels, direct_rank_rows(): pl.pallas_call(functools.partial(direct_act_kernel, nt, nz), in_specs=[vm...  28 us
    squeeze x4, local copies, waits for them, and re-layouts, reduce_rows(): give = lax.dynamic_index_in_dim(x, 1 - core, 1, keepdims=False)  7.93 us
    ppermute x4, waiting for transfers between devices, reduce_rows(): got = lax.ppermute(give, 'tensor', [(0, 1), (1, 0), (2, 3), (3, 2)])  7.38 us
  transfers between devices with their start and end apart: 10, of which 8 were waited for; matrix products, arithmetic and copies ran while one was open for 6% of the time, Pallas kernels for 27%

profile of v2, /device:TPU:0, one launch (start us, length us, event | category | flops | bytes accessed | tf_op | source)
XLA Modules:
  0.0 321.6 jit_solution(5970856408802202445)
XLA Ops:
  7.2 0.7 all-gather.3.cloned.1.call-update
  8.0 0.7 copy.24
  8.7 0.1 reduce
  8.9 0.1 convert_reduce_fusion
  8.9 0.7 select_reduce_fusion.1
  9.7 1.0 copy.26.adapter_ref
  10.7 0.8 select_reduce_fusion
  11.5 0.3 fusion.12.keep_ref
  11.8 81.2 %all-gather.3.cloned.1.call-done.x_ref = bf16[1024,2048]{1,0:T(8,128)(2,1)} async-done(((bf16[256,2048]{1,0:T(8,128)(2,1)}), bf16[1024,2048]{1,0:T(8,128)(2,1)}) %all-gather.3.cloned.1.call-update) | async-done | bytes 4194320 | tf_op jit(solution)/shard_map/all_gather | solution.py:354
  93.1 24.3 %shard_map.148.low_ref = f32[1024,192]{1,0:T(8,128)} custom-call(s32[1]{0:T(128)} %bitcast.3.first_ref, s32[1024,1]{1,0:T(8,128)} %copy.26.adapter_ref, bf16[1024,2048]{1,0:T(8,128)(2,1)} %all-gather.3.cloned.1.call-done.x_ref, bf16[16,192,2048]{2,1,0:T(8,128)(2,1)} %bitcast.83), custom_call_target="tpu_custom_call" | custom-call | flops 12884901888 | bytes 16777216 | tf_op jit(solution)/shard_map/pallas_call | solution.py:42
  117.4 1.2 copy-done
  118.6 34.1 %shard_map.149 = bf16[1024,192]{1,0:T(8,128)(2,1)S(1)} custom-call(f32[1024,192]{1,0:T(8,128)S(1)} %copy-done, f32[1024,64]{1,0:T(8,128)S(1)} %fusion.12.keep_ref), custom_call_target="tpu_custom_call" | custom-call | bytes 41943040 | tf_op jit(solution)/shard_map/pallas_call | solution.py:134
  152.7 0.9 slice_select_fusion
  153.6 18.8 %shard_map.150 = bf16[1024,2048]{1,0:T(8,128)(2,1)} custom-call(s32[1]{0:T(128)} %bitcast.first_ref, s32[1024,1]{1,0:T(8,128)} %copy.26.adapter_ref, bf16[1024,2048]{1,0:T(8,128)(2,1)} %all-gather.3.cloned.1.call-done.x_ref, bf16[1024,64]{1,0:T(8,128)(2,1)} %get-tuple-element.14.rank_ref, bf16[2048,2048]{1,0:T(8,128)(2,1)} %w_ref.4, bf16[1024,2048]{1,0:T(8,128)(2,1)} %bitcast.84), custom_call_target="tpu_custom_call" | custom-call | flops 12884901888 | bytes 20971520 | tf_op jit(solution)/shard_map/pallas_call | solution.py:268
  172.3 3.2 dynamic-slice_bitcast_fusion
  175.5 0.3 collective-permute-start
  175.8 4.1 %collective-permute-done = bf16[2,256,2048]{2,1,0:T(8,128)(2,1)S(1)} collective-permute-done((bf16[2,256,2048]{2,1,0:T(8,128)(2,1)}, bf16[2,256,2048]{2,1,0:T(8,128)(2,1)S(1)}, u32[]{:S(2)}, u32[]{:S(2)}) %collective-permute-start) | collective-permute-done | bytes 2097184 | tf_op jit(solution)/shard_map/ppermute | solution.py:317
  179.9 2.6 fusion
  182.5 1.4 collective-permute-start.1
  183.9 8.3 %shard_map.151 = bf16[1024,512]{1,0:T(8,128)(2,1)} custom-call(s32[1]{0:T(128)} %bitcast.first_ref, s32[1024,1]{1,0:T(8,128)} %copy.26.adapter_ref, bf16[1024,2048]{1,0:T(8,128)(2,1)} %all-gather.3.cloned.1.call-done.x_ref, bf16[1024,64]{1,0:T(8,128)(2,1)} %get-tuple-element.13.rank_ref, bf16[2048,512]{1,0:T(8,128)(2,1)} %w_ref.5, bf16[1024,512]{1,0:T(8,128)(2,1)} %bitcast.88), custom_call_target="tpu_custom_call" | custom-call | flops 3221225472 | bytes 8388608 | tf_op jit(solution)/shard_map/pallas_call | solution.py:268
  192.2 1.9 dynamic-slice_bitcast_fusion.3
  194.1 2.1 collective-permute-done.2
  196.2 1.0 fusion.9
  197.2 11.0 %collective-permute-done.1 = bf16[256,2048]{1,0:T(8,128)(2,1)} collective-permute-done((bf16[256,2048]{1,0:T(8,128)(2,1)}, bf16[256,2048]{1,0:T(8,128)(2,1)}, u32[]{:S(2)}, u32[]{:S(2)}) %collective-permute-start.1) | collective-permute-done | bytes 1048608 | tf_op jit(solution)/shard_map/ppermute | solution.py:325
  208.2 3.1 fusion.2
  211.2 9.0 %shard_map.152.low_ref = f32[1024,64]{1,0:T(8,128)} custom-call(s32[1]{0:T(128)} %bitcast.3.first_ref, s32[1024,1]{1,0:T(8,128)} %copy.26.adapter_ref, bf16[1024,2048]{1,0:T(8,128)(2,1)} %all-gather.5.cloned.1.call-done.x_ref, bf16[16,64,2048]{2,1,0:T(8,128)(2,1)} %bitcast.85), custom_call_target="tpu_custom_call" | custom-call | flops 4294967296 | bytes 8388608 | tf_op jit(solution)/shard_map/pallas_call | solution.py:42
  220.2 1.0 copy-done.1
  221.3 28.0 %shard_map.153.rank_ref = bf16[1024,64]{1,0:T(8,128)(2,1)S(1)} custom-call(f32[1024,64]{1,0:T(8,128)S(1)} %copy-done.1, f32[1024,64]{1,0:T(8,128)S(1)} %fusion.12.keep_ref), custom_call_target="tpu_custom_call" | custom-call | bytes 41943040 | tf_op jit(solution)/shard_map/pallas_call | solution.py:223
  249.3 0.7 copy-done.2
  250.0 11.9 %shard_map.154 = bf16[1024,1024]{1,0:T(8,128)(2,1)} custom-call(s32[1]{0:T(128)} %bitcast.first_ref, s32[1024,1]{1,0:T(8,128)} %copy.26.adapter_ref, bf16[1024,2048]{1,0:T(8,128)(2,1)} %all-gather.5.cloned.1.call-done.x_ref, bf16[1024,64]{1,0:T(8,128)(2,1)} %copy-done.2, bf16[2048,2048]{1,0:T(8,128)(2,1)} %w_ref.7, bf16[1024,2048]{1,0:T(8,128)(2,1)} %bitcast.86), custom_call_target="tpu_custom_call" | custom-call | flops 6442450944 | bytes 12582912 | tf_op jit(solution)/shard_map/pallas_call | solution.py:268
  261.9 1.4 dynamic-slice_bitcast_fusion.2
  263.4 0.8 collective-permute-start.4
  264.1 1.3 collective-permute-start.3
  265.5 7.0 %collective-permute-done.3 = bf16[256,512]{1,0:T(8,128)(2,1)S(1)} collective-permute-done((bf16[256,512]{1,0:T(8,128)(2,1)S(1)}, bf16[256,512]{1,0:T(8,128)(2,1)S(1)}, u32[]{:S(2)}, u32[]{:S(2)}) %collective-permute-start.3) | collective-permute-done | bytes 262176 | tf_op jit(solution)/shard_map/ppermute | solution.py:325
  272.4 1.8 fusion.11
  274.2 0.2 fusion.6
  274.4 11.9 %shard_map.155 = bf16[1024,1024]{1,0:T(8,128)(2,1)} custom-call(s32[1]{0:T(128)} %bitcast.first_ref, s32[1024,1]{1,0:T(8,128)} %copy.26.adapter_ref, bf16[1024,2048]{1,0:T(8,128)(2,1)} %all-gather.5.cloned.1.call-done.x_ref, bf16[1024,64]{1,0:T(8,128)(2,1)} %copy-done.2, bf16[2048,2048]{1,0:T(8,128)(2,1)} %w_ref.7, bf16[1024,2048]{1,0:T(8,128)(2,1)} %bitcast.87), custom_call_target="tpu_custom_call" | custom-call | flops 6442450944 | bytes 12582912 | tf_op jit(solution)/shard_map/pallas_call | solution.py:268
  286.3 1.4 dynamic-slice_bitcast_fusion.1
  287.8 0.1 collective-permute-start.6
  287.8 1.4 collective-permute-start.5
  289.3 1.2 collective-permute-done.6
  290.5 0.2 fusion.3
  290.7 1.4 collective-permute-start.7
  292.1 10.5 %collective-permute-done.5 = bf16[256,1024]{1,0:T(8,128)(2,1)S(1)} collective-permute-done((bf16[256,1024]{1,0:T(8,128)(2,1)S(1)}, bf16[256,1024]{1,0:T(8,128)(2,1)S(1)}, u32[]{:S(2)}, u32[]{:S(2)}) %collective-permute-start.5) | collective-permute-done | bytes 524320 | tf_op jit(solution)/shard_map/ppermute | solution.py:325
  302.6 0.3 fusion.8
  302.9 10.5 %collective-permute-done.7 = bf16[256,1024]{1,0:T(8,128)(2,1)S(1)} collective-permute-done((bf16[256,1024]{1,0:T(8,128)(2,1)S(1)}, bf16[256,1024]{1,0:T(8,128)(2,1)S(1)}, u32[]{:S(2)}, u32[]{:S(2)}) %collective-permute-start.7) | collective-permute-done | bytes 524320 | tf_op jit(solution)/shard_map/ppermute | solution.py:325
  313.4 0.3 fusion.5
  313.7 1.1 pad_maximum_fusion
  (15 shorter events, 0.2 us)
Async XLA Ops:
  7.2 85.9 %all-gather.3.cloned.1.call-start = ((), (), s32[]{:S(2)}) async-start(), calls=%async_computation | async-start | bytes 5242880 | tf_op jit(solution)/shard_map/all_gather | solution.py:354
  7.9 203.3 %all-gather.5.cloned.1.call-start = ((), (), s32[]{:S(2)}) async-start(), calls=%async_computation.1 | async-start | bytes 5242880 | tf_op jit(solution)/shard_map/all_gather | solution.py:354
  117.4 1.2 copy-start
  175.5 4.4 %collective-permute-start = (bf16[2,256,2048]{2,1,0:T(8,128)(2,1)}, bf16[2,256,2048]{2,1,0:T(8,128)(2,1)S(1)}, u32[]{:S(2)}, u32[]{:S(2)}) collective-permute-start(bf16[2,256,2048]{2,1,0:T(8,128)(2,1)} %dynamic-slice_bitcast_fusion), channel_id=1, source_target_pairs={{0,4},{4,0},{8,12},{12,8},{1,5},{5,1},{9,13},{13,9},{2,6},{6,2},{1... | collective-permute-start | bytes 6291464 | tf_op jit(solution)/shard_map/ppermute | solution.py:317
  182.5 25.7 %collective-permute-start.1 = (bf16[256,2048]{1,0:T(8,128)(2,1)}, bf16[256,2048]{1,0:T(8,128)(2,1)}, u32[]{:S(2)}, u32[]{:S(2)}) collective-permute-start(bf16[256,2048]{1,0:T(8,128)(2,1)} %fusion), channel_id=1, source_target_pairs={{0,8},{8,0},{4,12},{12,4},{1,9},{9,1},{5,13},{13,5},{2,10},{10,2},... | collective-permute-start | bytes 3145736 | tf_op jit(solution)/shard_map/ppermute | solution.py:325
  194.1 2.1 collective-permute-start.2
  220.2 1.0 copy-start.1
  249.3 0.7 copy-start.2
  261.9 12.3 %copy-start.3 = (bf16[1024,1024]{1,0:T(8,128)(2,1)S(1)}, bf16[1024,1024]{1,0:T(8,128)(2,1)}, u32[]{:S(2)}) copy-start(bf16[1024,1024]{1,0:T(8,128)(2,1)} %shard_map.154) | copy-start | bytes 6291460
  263.4 10.8 %collective-permute-start.4 = (bf16[2,256,1024]{2,1,0:T(8,128)(2,1)S(1)}, bf16[2,256,1024]{2,1,0:T(8,128)(2,1)S(1)}, u32[]{:S(2)}, u32[]{:S(2)}) collective-permute-start(bf16[2,256,1024]{2,1,0:T(8,128)(2,1)S(1)} %dynamic-slice_bitcast_fusion.2), channel_id=1, source_target_pairs={{0,4},{4,0},{8,12},{12,8},{1,5},{5,1},{9,13},{13,9},{2,6},{6,2},{1... | collective-permute-start | bytes 3145736 | tf_op jit(solution)/shard_map/ppermute | solution.py:317
  264.1 8.3 %collective-permute-start.3 = (bf16[256,512]{1,0:T(8,128)(2,1)S(1)}, bf16[256,512]{1,0:T(8,128)(2,1)S(1)}, u32[]{:S(2)}, u32[]{:S(2)}) collective-permute-start(bf16[256,512]{1,0:T(8,128)(2,1)S(1)} %fusion.9), channel_id=1, source_target_pairs={{0,8},{8,0},{4,12},{12,4},{1,9},{9,1},{5,13},{13,5},{2,10},{10,2},... | collective-permute-start | bytes 786440 | tf_op jit(solution)/shard_map/ppermute | solution.py:325
  286.3 4.2 %copy-start.4 = (bf16[1024,1024]{1,0:T(8,128)(2,1)S(1)}, bf16[1024,1024]{1,0:T(8,128)(2,1)}, u32[]{:S(2)}) copy-start(bf16[1024,1024]{1,0:T(8,128)(2,1)} %shard_map.155) | copy-start | bytes 6291460
  287.8 2.7 collective-permute-start.6
  287.8 14.8 %collective-permute-start.5 = (bf16[256,1024]{1,0:T(8,128)(2,1)S(1)}, bf16[256,1024]{1,0:T(8,128)(2,1)S(1)}, u32[]{:S(2)}, u32[]{:S(2)}) collective-permute-start(bf16[256,1024]{1,0:T(8,128)(2,1)S(1)} %fusion.6), channel_id=1, source_target_pairs={{0,8},{8,0},{4,12},{12,4},{1,9},{9,1},{5,13},{13,5},{2,10},{10,2},... | collective-permute-start | bytes 1572872 | tf_op jit(solution)/shard_map/ppermute | solution.py:325
  290.7 22.7 %collective-permute-start.7 = (bf16[256,1024]{1,0:T(8,128)(2,1)S(1)}, bf16[256,1024]{1,0:T(8,128)(2,1)S(1)}, u32[]{:S(2)}, u32[]{:S(2)}) collective-permute-start(bf16[256,1024]{1,0:T(8,128)(2,1)S(1)} %fusion.3), channel_id=1, source_target_pairs={{0,8},{8,0},{4,12},{12,4},{1,9},{9,1},{5,13},{13,5},{2,10},{10,2},... | collective-permute-start | bytes 1572872 | tf_op jit(solution)/shard_map/ppermute | solution.py:325
Sparse Core Ops, SparseCore 0:
  9.6 83.4 all-gather.2
  94.6 90.3 all-gather.4
